TPU v7x, 32 devices: a whole 2x2x4 slice. The times are simulated.
32 devices in a mesh: tile: 8 (over z, x), kern: 4 (over y, core).
Axes of the slice: x: 2, y: 2, z: 4, core: 2. Of those that a mesh axis runs over, the one named last changes fastest.
Arguments:
- mask_logit: float32 [1024, 256], P('tile'), may hold values from -6 to 6
- target: int32 [1024, 256], P('tile'), may hold values 0 or 1
- kern_real: float32 [12, 65, 65], P('kern'), may hold values from -0.09375 to 0.09375
- kern_imag: float32 [12, 65, 65], P('kern'), may hold values from -0.09375 to 0.09375
- kern_weight: float32 [12], P('kern'), may hold values from 0.07 to 0.14
Outputs:
- logit_grad: float32 [1024, 256], P('tile', 'kern')
All inputs are finite; a program needn't handle non-finite values. No bound on the sum of `target` on one device may be relied on, other than what follows from the above.
Results may differ from a plain program's by a relative error of at most 0.00021.
Values sent between devices are 32-bit elements; how exact they have to be, the bound alone decides.
No kernel may reach another device: no remote copies, remote signals or barrier semaphores. Data moves between devices by JAX's collectives and lax.ppermute only.
A program may use at most 64 MiB of HBM per device.

v0:
```python
import functools
import math

import jax
import jax.numpy as jnp
from jax import lax
from jax.experimental import pallas as pl
from jax.experimental.pallas import tpu as pltpu
from jax.sharding import PartitionSpec as P

MASK_SLOPE = 3.0
RESIST_SLOPE = 6.0
RESIST_LEVEL = 1.0

STEP = 64
SIZE = 128
TAP_ROWS = 72

F32 = jnp.float32
BF16 = jnp.bfloat16
TABLE_ROWS = (384, 512, 256, 512, 256, 256, 512, 256, 256)
BUFFERS = 3


def table_views(ref):
    views, at = [], 0
    for rows in TABLE_ROWS:
        views.append(ref.at[at:at + rows])
        at += rows
    return views


def split(value):
    high = value.astype(BF16)
    return high, (value - high.astype(F32)).astype(BF16)


def dot(left, right):
    return jnp.dot(left, right, preferred_element_type=F32)


def own_window(logit, place):
    cols = logit.shape[1]
    start = (place - 1) * STEP
    turned = pltpu.roll(jax.nn.sigmoid(MASK_SLOPE * logit), lax.rem(2 * cols - start, cols), 1)
    at = lax.broadcasted_iota(jnp.int32, logit.shape, 1) + start
    return jnp.where((at >= 0) & (at < cols), turned, 0.0)


def own_target(target, place):
    cols = target.shape[1]
    start = place * STEP - STEP // 2
    return pltpu.roll(target.astype(F32), lax.rem(2 * cols - start, cols), 1)[:, :SIZE]


def left_dot(table, value):
    rows = table.shape[0] // 2
    high, low = value
    both = dot(table[...], high)
    return both[:rows] + (both[rows:] + dot(table[0:rows], low))


def unit_waves():
    row = lax.broadcasted_iota(jnp.int32, (SIZE, SIZE), 0)
    col = lax.broadcasted_iota(jnp.int32, (SIZE, SIZE), 1)
    phase = (row * col) & (SIZE - 1)
    quarter = (phase + SIZE // 8) >> (SIZE.bit_length() - 3)
    rest = phase - quarter * (SIZE // 4)
    angle = rest.astype(F32) * (2.0 * math.pi / SIZE)
    square = angle * angle
    sin_near = cos_near = jnp.ones_like(angle)
    for step in (8, 6, 4, 2):
        sin_near = 1.0 - square * (1.0 / (step * (step + 1))) * sin_near
    for step in (10, 8, 6, 4, 2):
        cos_near = 1.0 - square * (1.0 / (step * (step - 1))) * cos_near
    sin_near = sin_near * angle
    turned = (quarter & 1) == 1
    cos_all = jnp.where(turned, -sin_near, cos_near)
    sin_all = jnp.where(turned, cos_near, sin_near)
    flip = (quarter & 2) == 2
    return jnp.where(flip, -cos_all, cos_all), jnp.where(flip, -sin_all, sin_all)


def table_kernel(table_ref):
    (
        taps_cols, taps_rows, mask_cols, rows_fwd, rows_inv, cols_inv, cols_fwd, grad_rows, grad_cols
    ) = table_views(table_ref)
    cos, sin = unit_waves()
    lane = lax.broadcasted_iota(jnp.int32, (SIZE, SIZE), 1)
    row = lax.broadcasted_iota(jnp.int32, (SIZE, SIZE), 0)
    left = lane < STEP
    scale = 1.0 / SIZE
    near, far = slice(0, STEP), slice(STEP, SIZE)

    def put(ref, blocks):
        rows = ref.shape[0] // 2
        at = 0
        for first, second in blocks:
            for column, value in enumerate((first, second)):
                for base, part in zip((0, rows), split(value)):
                    span = slice(column * SIZE, (column + 1) * SIZE)
                    ref[base + at:base + at + value.shape[0], span] = part
            at += first.shape[0]

    put(taps_cols.at[0:2 * SIZE], ((cos[near], sin[near]), (-sin[near], cos[near])))
    sign = (1 - 2 * (lane & 1)).astype(F32)
    even = (row & 1) == 0
    taps_cols[2 * SIZE:, :SIZE] = jnp.where(even, sign, 0.0).astype(BF16)
    taps_cols[2 * SIZE:, SIZE:] = jnp.where(even, 0.0, sign).astype(BF16)
    live = lane < SIZE - STEP + 1
    held = [[part.astype(F32) for part in split(jnp.where(live, wave, 0.0))] for wave in (cos, sin)]
    (cos_high, cos_low), (sin_high, sin_low) = held
    for phase, parts in enumerate((
        (cos_high, -sin_high, cos_high, -sin_high, cos_low, -sin_low),
        (sin_high, cos_high, sin_high, cos_high, sin_low, cos_low),
    )):
        for block in range(4):
            value = jnp.zeros((SIZE, SIZE), F32)
            for index, part in enumerate(parts):
                shift = index * TAP_ROWS - block * SIZE
                if -TAP_ROWS < shift < SIZE:
                    moved = pltpu.roll(part, shift % SIZE, 1) if shift % SIZE else part
                    value = jnp.where((lane >= shift) & (lane < shift + TAP_ROWS), moved, value)
            base = (block // 2) * 2 * SIZE + phase * SIZE
            span = slice((block % 2) * SIZE, (block % 2 + 1) * SIZE)
            taps_rows[base:base + SIZE, span] = value.astype(BF16)
    put(mask_cols, ((cos, -sin),))
    put(rows_fwd, ((cos, sin), (-sin, cos)))
    cos_s, sin_s = cos * scale, sin * scale
    put(rows_inv, ((cos_s[near], -sin_s[near]), (sin_s[near], cos_s[near])))
    cos_r, sin_r = pltpu.roll(cos_s, STEP, 1), pltpu.roll(sin_s, STEP, 1)
    for phase, value in enumerate((
        jnp.where(left, cos_s, sin_r), jnp.where(left, -sin_s, cos_r)
    )):
        for column, part in enumerate(split(value)):
            span = slice(column * SIZE, (column + 1) * SIZE)
            cols_inv[phase * SIZE:(phase + 1) * SIZE, span] = part
    put(cols_fwd, [
        pair for half in (near, far) for pair in ((cos[half], -sin[half]), (sin[half], cos[half]))
    ])
    put(grad_rows, ((cos_s[far], -sin_s[far]), (sin_s[far], cos_s[far])))
    for phase, (moved, value) in enumerate(((cos_r, cos_s), (-sin_r, -sin_s))):
        both = jnp.where(left, split(moved)[0].astype(F32), split(value)[1].astype(F32))
        grad_cols[phase * SIZE:(phase + 1) * SIZE, :SIZE] = both.astype(BF16)
        grad_cols[phase * SIZE:(phase + 1) * SIZE, SIZE:] = jnp.zeros((SIZE, SIZE), BF16)


def pack_kernel(weight_ref, logit_ref, target_ref, real_ref, imag_ref, even_ref, odd_ref, taps_ref):
    rows = logit_ref.shape[0]
    reach = SIZE - STEP
    half = reach // 2
    place = lax.axis_index("kern")
    to_next = lax.rem(lax.axis_index("tile"), 2) == 0
    window = own_window(logit_ref[...], place)
    wanted = own_target(target_ref[...], place)

    def packed(ref, near, near_target):
        ref[0:reach] = near[:, :SIZE]
        ref[reach:reach + half, :STEP] = near[:half, SIZE:SIZE + STEP]
        ref[reach:reach + half, STEP:] = near[half:, SIZE:SIZE + STEP]
        ref[reach + half:] = near_target

    top = window[0:reach]
    bottom = window[rows - reach:]
    top_target = wanted[0:half]
    bottom_target = wanted[rows - half:]
    packed(even_ref, jnp.where(to_next, bottom, top), jnp.where(to_next, bottom_target, top_target))
    packed(odd_ref, jnp.where(to_next, top, bottom), jnp.where(to_next, top_target, bottom_target))

    count = real_ref.shape[1]
    sublane = lax.broadcasted_iota(jnp.int32, (count, count), 0)
    lane = lax.broadcasted_iota(jnp.int32, (count, count), 1)
    taps_ref[...] = jnp.zeros_like(taps_ref)
    for kernel in range(real_ref.shape[0]):
        root = jnp.sqrt(jnp.full((1, count), weight_ref[kernel], F32))
        for part, ref in enumerate((real_ref, imag_ref)):
            taps = ref[kernel] * root
            taps_ref[kernel, 0:count, part * STEP:(part + 1) * STEP] = taps[:, :STEP]
            last = jnp.where(sublane == lane, taps[:, STEP:STEP + 1], 0.0)
            taps_ref[kernel, count + part:count + part + 1, 0:count] = jnp.sum(
                last, axis=0, keepdims=True
            )


def right_dot(value, table):
    high, low = split(value)
    rows = table.shape[0] // 2
    whole = jnp.concatenate([table[0:rows], table[0:rows], table[rows:]], axis=0)
    return dot(jnp.concatenate([high, low, high], axis=1), whole)


def tap_columns(blocks, work_t, taps_cols):
    tap_rows = blocks[0].shape[0]
    tap_count = SIZE - STEP + 1
    ends = [block[tap_count:tap_count + 2] for block in blocks]
    ends.append(jnp.zeros((STEP - 2 * len(blocks), SIZE), F32))
    ends = jnp.concatenate(ends, axis=0)
    turned = jnp.transpose(jnp.concatenate([ends, ends], axis=0))[:tap_rows]
    lane = lax.broadcasted_iota(jnp.int32, turned.shape, 1)
    coarse = turned.astype(BF16).astype(F32)
    turned = jnp.where(lane < STEP, coarse, turned - coarse)
    owner = (lane & (STEP - 1)) >> 1
    for index, block in enumerate(blocks):
        part = slice(index * tap_rows, (index + 1) * tap_rows)
        high, low = split(block)
        work_t[part, 0:128] = high
        work_t[part, 128:256] = low
        work_t[part, 256:384] = high
        work_t[part, 384:512] = jnp.where(owner == index, turned, 0.0).astype(BF16)
    table = [taps_cols[at * SIZE:(at + 1) * SIZE] for at in (0, 0, 1, 2)]
    return dot(work_t[0:len(blocks) * tap_rows], jnp.concatenate(table, axis=0))


def tap_spectra(mixed, indices, taps_rows, store):
    columns = []
    for index in indices:
        part = slice(index * TAP_ROWS, (index + 1) * TAP_ROWS)
        columns.append(jnp.concatenate([mixed[part, :SIZE], mixed[part, SIZE:]], axis=0))
    high, low = split(jnp.concatenate(columns, axis=1))
    wide = jnp.concatenate([taps_rows[0:2 * SIZE], taps_rows[2 * SIZE:]], axis=1)
    spectra = dot(wide[:, :6 * TAP_ROWS], jnp.concatenate([high, low, high], axis=0))
    for place, index in enumerate(indices):
        store(index, spectra[:, place * SIZE:(place + 1) * SIZE])


def field_products(spectrum, mask_spec, work, slot):
    for side in range(2):
        cut = slice(side * SIZE, (side + 1) * SIZE)
        to = slice((2 * slot + side) * SIZE, (2 * slot + side + 1) * SIZE)
        kern_re = spectrum[0:SIZE]
        kern_im = spectrum[SIZE:]
        mask_re = mask_spec[0:SIZE, cut]
        mask_im = mask_spec[SIZE:, cut]
        high, low = split(mask_re * kern_re - mask_im * kern_im)
        work[0, 0:SIZE, to] = high
        work[1, 0:SIZE, to] = low
        high, low = split(mask_re * kern_im + mask_im * kern_re)
        work[0, SIZE:, to] = high
        work[1, SIZE:, to] = low


def field_rows_step(work, work_z, windows, rows_inv):
    width = windows * 2 * SIZE
    high, low = split(left_dot(rows_inv, (work[0, :, 0:width], work[1, :, 0:width])))
    for piece in range(windows * 2):
        cut = slice(piece * SIZE, (piece + 1) * SIZE)
        at = slice(piece * STEP, (piece + 1) * STEP)
        work_z[0, at, 0:SIZE] = high[0:STEP, cut]
        work_z[0, at, SIZE:] = high[STEP:, cut]
        work_z[1, at, 0:SIZE] = low[0:STEP, cut]
        work_z[1, at, SIZE:] = low[STEP:, cut]


def field_cols_step(work_z, windows, cols_inv):
    pieces = windows * 2
    major = dot(work_z[0, 0:pieces * STEP], cols_inv[...])
    minor = dot(work_z[1, 0:pieces * STEP], cols_inv[:, 0:SIZE])
    result = major[:, 0:SIZE] + (major[:, SIZE:] + minor)
    return [
        [result[(index * 2 + side) * STEP:(index * 2 + side + 1) * STEP] for side in range(2)]
        for index in range(windows)
    ]


def all_spectra(blocks, work_t, taps_cols, taps_rows, out):
    mixed = tap_columns(blocks, work_t, taps_cols)

    def store(index, value):
        out[index] = value

    for first in range(0, len(blocks), 2):
        tap_spectra(mixed, range(first, min(first + 2, len(blocks))), taps_rows, store)


def all_fields(todo, spectra, mask_specs, work_x, work_z, rows_inv, cols_inv, take):
    def products(at):
        kernel, windows = todo[at]
        for slot, window in enumerate(windows):
            field_products(spectra[kernel], mask_specs[window], work_x.at[at % BUFFERS], slot)

    products(0)
    for at in range(len(todo) + 1):
        if at + 1 < len(todo):
            products(at + 1)
        if at < len(todo):
            buffer = at % BUFFERS
            field_rows_step(work_x.at[buffer], work_z.at[buffer], len(todo[at][1]), rows_inv)
        if at > 0:
            kernel, windows = todo[at - 1]
            pieces = field_cols_step(work_z.at[(at - 1) % BUFFERS], len(windows), cols_inv)
            for index, pair in zip(windows, pieces):
                take(kernel, index, pair)


def local_kernel(
    logit_ref, taps0, taps1, taps2, table_ref,
    spectra, own_cols, mid_spec, mid_fields, mid_total,
    work_t, work_x, work_z,
):
    taps_cols, taps_rows, mask_cols, rows_fwd, rows_inv, cols_inv = table_views(table_ref)[:6]
    rows, cols = logit_ref.shape
    own = own_window(logit_ref[...], lax.axis_index("kern"))
    for side in range(2):
        window = own[:, :SIZE] if side == 0 else pltpu.roll(own, cols - STEP, 1)[:, :SIZE]
        mixed = right_dot(window, mask_cols)
        span = slice(side * SIZE, (side + 1) * SIZE)
        for half_at, part in enumerate(split(mixed)):
            own_cols[half_at, 0, :, span] = part[:, :SIZE]
            own_cols[half_at, 1, :, span] = part[:, SIZE:]
    mid_spec[...] = left_dot(
        rows_fwd,
        (own_cols[0].reshape(2 * rows, 2 * SIZE), own_cols[1].reshape(2 * rows, 2 * SIZE)),
    )
    blocks = [ref[kernel] for ref in (taps0, taps1, taps2) for kernel in range(ref.shape[0])]
    all_spectra(blocks, work_t, taps_cols, taps_rows, spectra)
    mid_total[...] = jnp.zeros_like(mid_total)

    def take(kernel, index, pair):
        for side, piece in enumerate(pair):
            cut = slice(side * SIZE, (side + 1) * SIZE)
            mid_fields[kernel, :, cut] = piece
            mid_total[:, cut] += piece * piece

    all_fields(
        [(kernel, (1,)) for kernel in range(len(blocks))],
        [spectra.at[kernel] for kernel in range(len(blocks))],
        {1: mid_spec}, work_x, work_z, rows_inv, cols_inv, take,
    )


def main_kernel(
    logit_ref, target_ref, even_ref, odd_ref, taps3, table_ref,
    early_spectra, own_cols, mid_spec, mid_fields, mid_total,
    out_ref,
    late_spectra, mask_spec, fields, total, slope, work_t, work_x, work_z, work_b, grad_spec,
):
    (
        taps_cols, taps_rows, mask_cols, rows_fwd, rows_inv, cols_inv, cols_fwd, grad_rows, grad_cols
    ) = table_views(table_ref)
    rows, cols = logit_ref.shape
    reach = SIZE - STEP
    half = reach // 2
    place = lax.axis_index("kern")
    band = lax.axis_index("tile")
    bands = lax.axis_size("tile")
    field_rows = rows + reach
    windows = field_rows // STEP
    outs = rows // STEP
    early = early_spectra.shape[0]
    late = taps3.shape[0]
    count = early + late
    pairs = count // 2
    spectra = [early_spectra.at[kernel] for kernel in range(early)]
    spectra += [late_spectra.at[kernel] for kernel in range(late)]

    even = lax.rem(band, 2) == 0
    above = jnp.where(even, odd_ref[...], even_ref[...])
    below = jnp.where(even, even_ref[...], odd_ref[...])
    lane = lax.broadcasted_iota(jnp.int32, (half, SIZE), 1)

    def second(block):
        outer = block[reach:reach + half]
        inner = pltpu.roll(block[0:reach], STEP, 1)
        return jnp.concatenate(
            [
                jnp.where(lane < STEP, inner[:half], pltpu.roll(outer, STEP, 1)),
                jnp.where(lane < STEP, inner[half:], outer),
            ],
            axis=0,
        )

    sides = (
        jnp.concatenate([above[0:reach], below[0:reach]], axis=0),
        jnp.concatenate([second(above), second(below)], axis=0),
    )
    for side, window in enumerate(sides):
        mixed = right_dot(window, mask_cols)
        for half_at, part in enumerate(split(mixed)):
            for phase in range(2):
                cut = slice(phase * SIZE, (phase + 1) * SIZE)
                base = phase * SIZE
                span = slice(side * SIZE, (side + 1) * SIZE)
                work_x[0, half_at, base:base + reach, span] = part[:reach, cut]
                span = slice((2 + side) * SIZE, (3 + side) * SIZE)
                work_x[0, half_at, base + STEP:base + SIZE, span] = part[reach:, cut]
    for half_at in range(2):
        for phase in range(2):
            base = phase * SIZE
            span = slice(0, 2 * SIZE)
            work_x[0, half_at, base + reach:base + SIZE, span] = own_cols[half_at, phase, 0:STEP]
            span = slice(2 * SIZE, 4 * SIZE)
            work_x[0, half_at, base:base + STEP, span] = own_cols[half_at, phase, rows - STEP:]
    outer = left_dot(rows_fwd, (work_x[0, 0, :, 0:4 * SIZE], work_x[0, 1, :, 0:4 * SIZE]))
    mask_spec[0] = outer[:, 0:2 * SIZE]
    mask_spec[1] = outer[:, 2 * SIZE:]

    all_spectra([taps3[kernel] for kernel in range(late)], work_t, taps_cols, taps_rows, late_spectra)

    total[0:STEP] = jnp.zeros((STEP, 2 * SIZE), F32)
    total[STEP:2 * STEP] = mid_total[...]
    total[2 * STEP:] = jnp.zeros((STEP, 2 * SIZE), F32)

    def take(kernel, index, pair):
        at_rows = slice(index * STEP, (index + 1) * STEP)
        for side, piece in enumerate(pair):
            cut = slice(side * SIZE, (side + 1) * SIZE)
            fields[kernel, at_rows, cut] = piece
            total[at_rows, cut] += piece * piece

    all_fields(
        [(kernel, (0, 2) if kernel < early else (0, 1, 2)) for kernel in range(count)],
        spectra, {0: mask_spec.at[0], 1: mid_spec, 2: mask_spec.at[1]},
        work_x, work_z, rows_inv, cols_inv, take,
    )

    def field(kernel):
        if kernel >= early:
            return fields[kernel]
        return jnp.concatenate(
            [fields[kernel, 0:STEP], mid_fields[kernel], fields[kernel, 2 * STEP:]], axis=0
        )

    target_near = jnp.concatenate(
        [above[reach + half:], own_target(target_ref[...], place), below[reach + half:]], axis=0
    )
    start = place * STEP - half
    target_turned = pltpu.roll(target_near, STEP, 1)
    lane = lax.broadcasted_iota(jnp.int32, (field_rows, SIZE), 1)
    row = lax.broadcasted_iota(jnp.int32, (field_rows, SIZE), 0) + band * rows - half
    first = lane < STEP
    low_lane = lane & (STEP - 1)
    for side in range(2):
        cut = slice(side * SIZE, (side + 1) * SIZE)
        squares = total[:, cut]
        intensity = squares + pltpu.roll(squares, STEP, 1)
        if side == 0:
            wanted = jnp.where(first, target_near, target_turned)
        else:
            wanted = jnp.where(first, target_turned, target_near)
        printed = jax.nn.sigmoid(RESIST_SLOPE * (intensity - RESIST_LEVEL))
        at = low_lane + (start + side * STEP)
        valid = (at >= 0) & (at < cols) & (row >= 0) & (row < bands * rows)
        slope[:, cut] = jnp.where(
            valid, (2.0 * RESIST_SLOPE) * (printed - wanted) * printed * (1.0 - printed), 0.0
        )

    grad_spec[...] = jnp.zeros_like(grad_spec)

    def grad_cols_step(pair):
        buffer = pair % BUFFERS
        value = jnp.concatenate(
            [slope[...] * field(2 * pair + member) for member in range(2)], axis=0
        )
        high, low = split(value)
        mixed = dot(high, cols_fwd[0:256]) + (
            dot(high, cols_fwd[256:]) + dot(low, cols_fwd[0:256])
        )
        for half_at, part in enumerate(split(mixed)):
            for index in range(outs):
                for member in range(2):
                    base = member * field_rows + index * STEP
                    at = slice(base, base + SIZE)
                    base = (2 * index + member) * SIZE
                    span = slice(base, base + SIZE)
                    work_b[buffer, half_at, 0:SIZE, span] = part[at, :SIZE]
                    work_b[buffer, half_at, SIZE:, span] = part[at, SIZE:]

    def grad_rows_step(pair):
        buffer = pair % BUFFERS
        spec = left_dot(rows_fwd, (work_b[buffer, 0], work_b[buffer, 1]))
        for index in range(outs):
            cut = slice(index * SIZE, (index + 1) * SIZE)
            sum_re = grad_spec[0:SIZE, cut]
            sum_im = grad_spec[SIZE:, cut]
            for member in range(2):
                base = (2 * index + member) * SIZE
                span = slice(base, base + SIZE)
                kern_re = spectra[2 * pair + member][0:SIZE]
                kern_im = spectra[2 * pair + member][SIZE:]
                spec_re = spec[0:SIZE, span]
                spec_im = spec[SIZE:, span]
                sum_re = sum_re + kern_re * spec_re + kern_im * spec_im
                sum_im = sum_im + kern_re * spec_im - kern_im * spec_re
            grad_spec[0:SIZE, cut] = sum_re
            grad_spec[SIZE:, cut] = sum_im

    for pair in range(pairs + 1):
        if pair < pairs:
            grad_cols_step(pair)
        if pair > 0:
            grad_rows_step(pair - 1)

    halfway = left_dot(grad_rows, split(grad_spec[...]))
    stacked = jnp.concatenate(
        [
            jnp.concatenate(
                [
                    halfway[0:STEP, index * SIZE:(index + 1) * SIZE],
                    halfway[STEP:, index * SIZE:(index + 1) * SIZE],
                ],
                axis=1,
            )
            for index in range(outs)
        ],
        axis=0,
    )
    high, low = split(stacked)
    both = dot(high, grad_cols[:, :SIZE])
    gradient = both[:, :STEP] + (both[:, STEP:] + dot(low, grad_cols[:, :STEP]))
    mask_share = pltpu.roll(
        jax.nn.sigmoid(MASK_SLOPE * logit_ref[...]), lax.rem(cols - place * STEP, cols), 1
    )[:, :STEP]
    out_ref[...] = jnp.transpose(
        gradient * (2.0 * MASK_SLOPE) * mask_share * (1.0 - mask_share)
    )


def body(mask_logit, target, kern_real, kern_imag, kern_weight):
    rows, cols = mask_logit.shape
    local, tap_count, _ = kern_real.shape
    reach = tap_count - 1
    kern_size = lax.axis_size("kern")
    tile_size = lax.axis_size("tile")
    assert reach == SIZE - STEP and cols == STEP * kern_size and rows % STEP == 0
    assert kern_size == 4 and rows == SIZE
    half = reach // 2
    vmem = pl.BlockSpec(memory_space=pltpu.VMEM)
    smem = pl.BlockSpec(memory_space=pltpu.SMEM)


    even, odd, taps = pl.pallas_call(
        pack_kernel,
        out_shape=(
            jax.ShapeDtypeStruct((2 * reach, SIZE), F32),
            jax.ShapeDtypeStruct((2 * reach, SIZE), F32),
            jax.ShapeDtypeStruct((local, TAP_ROWS, SIZE), F32),
        ),
        in_specs=[smem] + [vmem] * 4,
        out_specs=(vmem,) * 3,
    )(kern_weight, mask_logit, target, kern_real, kern_imag)

    def swaps(first):
        return [p for i in range(first, tile_size - 1, 2) for p in ((i, i + 1), (i + 1, i))]

    def flipped(value, flip):
        return lax.ppermute(value, "kern", [(i, i ^ flip) for i in range(kern_size)])

    far = flipped(taps, 2)
    near = flipped(taps, 1)
    even = lax.ppermute(even, "tile", swaps(0))
    odd = lax.ppermute(odd, "tile", swaps(1))
    both = flipped(far, 1)

    table = pl.pallas_call(
        table_kernel,
        out_shape=jax.ShapeDtypeStruct((sum(TABLE_ROWS), 2 * SIZE), BF16),
        out_specs=vmem,
        compiler_params=pltpu.CompilerParams(vmem_limit_bytes=8 * 1024 * 1024),
        cost_estimate=pl.CostEstimate(flops=2 * 10**9, bytes_accessed=5 * 10**6, transcendentals=0),
    )()
    field_rows = rows + reach
    windows = field_rows // STEP
    outs = rows // STEP
    count = local * kern_size
    early = count - local
    local_out = pl.pallas_call(
        local_kernel,
        out_shape=(
            jax.ShapeDtypeStruct((early, 2 * SIZE, SIZE), F32),
            jax.ShapeDtypeStruct((2, 2, rows, 2 * SIZE), BF16),
            jax.ShapeDtypeStruct((2 * SIZE, 2 * SIZE), F32),
            jax.ShapeDtypeStruct((early, STEP, 2 * SIZE), F32),
            jax.ShapeDtypeStruct((STEP, 2 * SIZE), F32),
        ),
        in_specs=[vmem] * 5,
        out_specs=(vmem,) * 5,
        scratch_shapes=[
            pltpu.VMEM((early * TAP_ROWS, 4 * SIZE), BF16),
            pltpu.VMEM((BUFFERS, 2, 2 * SIZE, 2 * SIZE), BF16),
            pltpu.VMEM((BUFFERS, 2, 2 * STEP, 2 * SIZE), BF16),
        ],
        compiler_params=pltpu.CompilerParams(vmem_limit_bytes=16 * 1024 * 1024),
        cost_estimate=pl.CostEstimate(flops=4 * 10**9, bytes_accessed=5 * 10**6, transcendentals=0),
    )(mask_logit, taps, near, far, table)
    result = pl.pallas_call(
        main_kernel,
        out_shape=jax.ShapeDtypeStruct((STEP, rows), F32),
        in_specs=[vmem] * (6 + len(local_out)),
        out_specs=vmem,
        scratch_shapes=[
            pltpu.VMEM((local, 2 * SIZE, SIZE), F32),
            pltpu.VMEM((2, 2 * SIZE, 2 * SIZE), F32),
            pltpu.VMEM((count, field_rows, 2 * SIZE), F32),
            pltpu.VMEM((field_rows, 2 * SIZE), F32),
            pltpu.VMEM((field_rows, 2 * SIZE), F32),
            pltpu.VMEM((local * TAP_ROWS, 4 * SIZE), BF16),
            pltpu.VMEM((BUFFERS, 2, 2 * SIZE, 2 * windows * SIZE), BF16),
            pltpu.VMEM((BUFFERS, 2, 2 * windows * STEP, 2 * SIZE), BF16),
            pltpu.VMEM((BUFFERS, 2, 2 * SIZE, 2 * outs * SIZE), BF16),
            pltpu.VMEM((2 * SIZE, outs * SIZE), F32),
        ],
        compiler_params=pltpu.CompilerParams(vmem_limit_bytes=24 * 1024 * 1024),
    )(mask_logit, target, even, odd, both, table, *local_out)
    return jnp.transpose(result)


def solution(mesh):
    in_specs = (
        P("tile", None),
        P("tile", None),
        P("kern", None, None),
        P("kern", None, None),
        P("kern"),
    )
    out_specs = P("tile", "kern")
    return jax.shard_map(body, mesh=mesh, in_specs=in_specs, out_specs=out_specs, check_vma=False)
```

profile of v0, /device:TPU:19, one launch (start us, length us, event | category | flops | bytes accessed | tf_op | source)
XLA Modules:
  0.0 21.9 jit_solution(14812083607558609792)
XLA Ops:
  0.0 2.0 %shard_map.55 = (f32[128,128]{1,0:T(8,128)}, f32[128,128]{1,0:T(8,128)}, f32[3,72,128]{2,1,0:T(8,128)}) custom-call(f32[3]{0:T(128)} %weight_ref.1, f32[128,256]{1,0:T(8,128)} %logit_ref.5, s32[128,256]{1,0:T(8,128)} %target_ref.3, f32[3,65,65]{2,1,0:T(8,128)} %real_ref.1, f32[3,65,65]{2,1,0:T(8,128)} %imag_ref.1), custom_call_target="tpu_custom_call" | custom-call | tf_op jit(solution)/shard_map/pallas_call | solution.py:531
  2.0 1.2 %collective-permute-start.2 = (f32[3,72,128]{2,1,0:T(8,128)}, f32[3,72,128]{2,1,0:T(8,128)S(1)}, u32[]{:S(2)}, u32[]{:S(2)}) collective-permute-start(f32[3,72,128]{2,1,0:T(8,128)} %get-tuple-element.15.taps0), channel_id=1, source_target_pairs={{0,2},{1,3},{2,0},{3,1},{4,6},{5,7},{6,4},{7,5},{8,10},{9,11},{10,... | collective-permute-start | bytes 331784 | tf_op jit(solution)/shard_map/ppermute | solution.py:546
  3.2 1.0 %collective-permute-start.4 = (f32[3,72,128]{2,1,0:T(8,128)}, f32[3,72,128]{2,1,0:T(8,128)S(1)}, u32[]{:S(2)}, u32[]{:S(2)}) collective-permute-start(f32[3,72,128]{2,1,0:T(8,128)} %get-tuple-element.15.taps0), channel_id=1, source_target_pairs={{0,1},{1,0},{2,3},{3,2},{4,5},{5,4},{6,7},{7,6},{8,9},{9,8},{10,11... | collective-permute-start | bytes 331784 | tf_op jit(solution)/shard_map/ppermute | solution.py:546
  4.2 0.3 %collective-permute-start = (f32[128,128]{1,0:T(8,128)}, f32[128,128]{1,0:T(8,128)S(1)}, u32[]{:S(2)}, u32[]{:S(2)}) collective-permute-start(f32[128,128]{1,0:T(8,128)} %get-tuple-element.13), channel_id=1, source_target_pairs={{0,4},{4,0},{8,12},{12,8},{16,20},{20,16},{24,28},{28,24},{1,5},{5... | collective-permute-start | bytes 196616 | tf_op jit(solution)/shard_map/ppermute | solution.py:550
  4.4 0.0 copy-start
  4.4 0.0 copy-start.2
  4.4 4.3 %collective-permute-start.1 = (f32[128,128]{1,0:T(8,128)}, f32[128,128]{1,0:T(8,128)S(1)}, u32[]{:S(2)}, u32[]{:S(2)}) collective-permute-start(f32[128,128]{1,0:T(8,128)} %get-tuple-element.14), channel_id=1, source_target_pairs={{4,8},{8,4},{12,16},{16,12},{20,24},{24,20},{5,9},{9,5},{13,17},{1... | collective-permute-start | bytes 196616 | tf_op jit(solution)/shard_map/ppermute | solution.py:551
  8.7 0.4 %shard_map.56.table_ref = bf16[3200,256]{1,0:T(8,128)(2,1)S(1)} custom-call(), custom_call_target="tpu_custom_call" | custom-call | flops 2000000000 | bytes 5000000 | tf_op jit(solution)/shard_map/pallas_call | solution.py:554
  9.1 0.0 copy-start.1
  9.1 0.0 collective-permute-done.2.taps2
  9.1 0.6 %collective-permute-start.3 = (f32[3,72,128]{2,1,0:T(8,128)S(1)}, f32[3,72,128]{2,1,0:T(8,128)S(1)}, u32[]{:S(2)}, u32[]{:S(2)}) collective-permute-start(f32[3,72,128]{2,1,0:T(8,128)S(1)} %collective-permute-done.2.taps2), channel_id=1, source_target_pairs={{0,1},{1,0},{2,3},{3,2},{4,5},{5,4},{6,7},{7,6},{8,9},{9,8},{10,11... | collective-permute-start | bytes 331784 | tf_op jit(solution)/shard_map/ppermute | solution.py:546
  9.8 0.0 collective-permute-done.4.taps1
  9.8 0.0 copy-done
  9.8 0.0 copy-done.2
  9.8 2.8 %shard_map.57 = (f32[9,256,128]{2,1,0:T(8,128)S(1)}, bf16[2,2,128,256]{3,2,1,0:T(8,128)(2,1)S(1)}, f32[256,256]{1,0:T(8,128)S(1)}, f32[9,64,256]{2,1,0:T(8,128)S(1)}, f32[64,256]{1,0:T(8,128)S(1)}) custom-call(f32[128,256]{1,0:T(8,128)S(1)} %copy-done, f32[3,72,128]{2,1,0:T(8,128)S(1)} %copy-done.2, f32[3,72,128]{2,1,0:T(8,128)S(1)} %collective-permute-done.4.taps1, ...), custom_call_target="tpu_custom_call" | custom-call | flops 4000000000 | bytes 5000000 | tf_op jit(solution)/shard_map/pallas_call | solution.py:566
  12.6 0.0 collective-permute-done.even_ref
  12.6 0.0 collective-permute-done.1.odd_ref
  12.6 0.0 collective-permute-done.3.taps3
  12.6 0.0 copy-done.1
  12.6 9.3 %shard_map.58 = f32[64,128]{1,0:T(8,128)} custom-call(f32[128,256]{1,0:T(8,128)S(1)} %copy-done, s32[128,256]{1,0:T(8,128)S(1)} %copy-done.1, f32[128,128]{1,0:T(8,128)S(1)} %collective-permute-done.even_ref, f32[128,128]{1,0:T(8,128)S(1)} %collective-permute-done.1.odd_ref, f32[3,72,128]{2,1,0:T(8,128)S(1)} %collective-permute-done.3.taps3, ...), custom_call_target="tpu_custom_call" | custom-call | tf_op jit(solution)/shard_map/pallas_call | solution.py:585
Async XLA Ops:
  2.0 7.2 %collective-permute-start.2 = (f32[3,72,128]{2,1,0:T(8,128)}, f32[3,72,128]{2,1,0:T(8,128)S(1)}, u32[]{:S(2)}, u32[]{:S(2)}) collective-permute-start(f32[3,72,128]{2,1,0:T(8,128)} %get-tuple-element.15.taps0), channel_id=1, source_target_pairs={{0,2},{1,3},{2,0},{3,1},{4,6},{5,7},{6,4},{7,5},{8,10},{9,11},{10,... | collective-permute-start | bytes 331784 | tf_op jit(solution)/shard_map/ppermute | solution.py:546
  3.2 6.6 %collective-permute-start.4 = (f32[3,72,128]{2,1,0:T(8,128)}, f32[3,72,128]{2,1,0:T(8,128)S(1)}, u32[]{:S(2)}, u32[]{:S(2)}) collective-permute-start(f32[3,72,128]{2,1,0:T(8,128)} %get-tuple-element.15.taps0), channel_id=1, source_target_pairs={{0,1},{1,0},{2,3},{3,2},{4,5},{5,4},{6,7},{7,6},{8,9},{9,8},{10,11... | collective-permute-start | bytes 331784 | tf_op jit(solution)/shard_map/ppermute | solution.py:546
  4.2 8.4 %collective-permute-start = (f32[128,128]{1,0:T(8,128)}, f32[128,128]{1,0:T(8,128)S(1)}, u32[]{:S(2)}, u32[]{:S(2)}) collective-permute-start(f32[128,128]{1,0:T(8,128)} %get-tuple-element.13), channel_id=1, source_target_pairs={{0,4},{4,0},{8,12},{12,8},{16,20},{20,16},{24,28},{28,24},{1,5},{5... | collective-permute-start | bytes 196616 | tf_op jit(solution)/shard_map/ppermute | solution.py:550
  4.4 5.3 %copy-start = (f32[128,256]{1,0:T(8,128)S(1)}, f32[128,256]{1,0:T(8,128)}, u32[]{:S(2)}) copy-start(f32[128,256]{1,0:T(8,128)} %logit_ref.5) | copy-start | bytes 393220
  4.4 5.3 %copy-start.2 = (f32[3,72,128]{2,1,0:T(8,128)S(1)}, f32[3,72,128]{2,1,0:T(8,128)}, u32[]{:S(2)}) copy-start(f32[3,72,128]{2,1,0:T(8,128)} %get-tuple-element.15.taps0) | copy-start | bytes 331780
  4.4 8.2 %collective-permute-start.1 = (f32[128,128]{1,0:T(8,128)}, f32[128,128]{1,0:T(8,128)S(1)}, u32[]{:S(2)}, u32[]{:S(2)}) collective-permute-start(f32[128,128]{1,0:T(8,128)} %get-tuple-element.14), channel_id=1, source_target_pairs={{4,8},{8,4},{12,16},{16,12},{20,24},{24,20},{5,9},{9,5},{13,17},{1... | collective-permute-start | bytes 196616 | tf_op jit(solution)/shard_map/ppermute | solution.py:551
  9.1 3.5 %copy-start.1 = (s32[128,256]{1,0:T(8,128)S(1)}, s32[128,256]{1,0:T(8,128)}, u32[]{:S(2)}) copy-start(s32[128,256]{1,0:T(8,128)} %target_ref.3) | copy-start | bytes 393220
  9.1 3.5 %collective-permute-start.3 = (f32[3,72,128]{2,1,0:T(8,128)S(1)}, f32[3,72,128]{2,1,0:T(8,128)S(1)}, u32[]{:S(2)}, u32[]{:S(2)}) collective-permute-start(f32[3,72,128]{2,1,0:T(8,128)S(1)} %collective-permute-done.2.taps2), channel_id=1, source_target_pairs={{0,1},{1,0},{2,3},{3,2},{4,5},{5,4},{6,7},{7,6},{8,9},{9,8},{10,11... | collective-permute-start | bytes 331784 | tf_op jit(solution)/shard_map/ppermute | solution.py:546
where the time goes:
time: 22.1 us; the launch traced here: 21.9 us
  Pallas kernels  14.5 us (66%)
  starting transfers between devices  7.33 us (33%)
    pallas_call x1, Pallas kernels, body(): pl.pallas_call(main_kernel, out_shape=jax.ShapeDtypeStruct((STEP, rows),...  9.27 us
    ppermute x1, starting transfers between devices, body(): odd = lax.ppermute(odd, 'tile', swaps(1))  4.25 us
    ppermute x3, starting transfers between devices, flipped(): lax.ppermute(value, 'kern', [(i, i ^ flip) for i in range(kern_size)])  2.82 us
    pallas_call x1, Pallas kernels, body(): pl.pallas_call(local_kernel, out_shape=(jax.ShapeDtypeStruct((early, 2 *...  2.81 us
    pallas_call x1, Pallas kernels, body(): pl.pallas_call(pack_kernel, out_shape=(jax.ShapeDtypeStruct((2 * reach, S...  1.98 us
  transfers between devices with their start and end apart: 5, of which 0 were waited for; matrix products, arithmetic and copies ran while one was open for 0% of the time, Pallas kernels for 15%

commit v1 on v0

--- a/solution.py
+++ b/solution.py
@@ -223,28 +223,27 @@
         store(index, spectra[:, place * SIZE:(place + 1) * SIZE])
 
 
-def field_products(spectrum, mask_spec, work, slot):
+def field_products(spectrum, mask_spec, work):
     for side in range(2):
         cut = slice(side * SIZE, (side + 1) * SIZE)
-        to = slice((2 * slot + side) * SIZE, (2 * slot + side + 1) * SIZE)
         kern_re = spectrum[0:SIZE]
         kern_im = spectrum[SIZE:]
         mask_re = mask_spec[0:SIZE, cut]
         mask_im = mask_spec[SIZE:, cut]
         high, low = split(mask_re * kern_re - mask_im * kern_im)
-        work[0, 0:SIZE, to] = high
-        work[1, 0:SIZE, to] = low
+        work[0, 0:SIZE, cut] = high
+        work[1, 0:SIZE, cut] = low
         high, low = split(mask_re * kern_im + mask_im * kern_re)
-        work[0, SIZE:, to] = high
-        work[1, SIZE:, to] = low
-
-
-def field_rows_step(work, work_z, windows, rows_inv):
-    width = windows * 2 * SIZE
-    high, low = split(left_dot(rows_inv, (work[0, :, 0:width], work[1, :, 0:width])))
-    for piece in range(windows * 2):
-        cut = slice(piece * SIZE, (piece + 1) * SIZE)
-        at = slice(piece * STEP, (piece + 1) * STEP)
+        work[0, SIZE:, cut] = high
+        work[1, SIZE:, cut] = low
+
+
+def field_rows_step(work, work_z, index, rows_inv):
+    high, low = split(left_dot(rows_inv, (work[0], work[1])))
+    for side in range(2):
+        cut = slice(side * SIZE, (side + 1) * SIZE)
+        base = (index * 2 + side) * STEP
+        at = slice(base, base + STEP)
         work_z[0, at, 0:SIZE] = high[0:STEP, cut]
         work_z[0, at, SIZE:] = high[STEP:, cut]
         work_z[1, at, 0:SIZE] = low[0:STEP, cut]
@@ -273,18 +272,23 @@
 
 
 def all_fields(todo, spectra, mask_specs, work_x, work_z, rows_inv, cols_inv, take):
-    def products(at):
+    def products(at, slot):
         kernel, windows = todo[at]
-        for slot, window in enumerate(windows):
-            field_products(spectra[kernel], mask_specs[window], work_x.at[at % BUFFERS], slot)
-
-    products(0)
+        field_products(
+            spectra[kernel], mask_specs[windows[slot]], work_x.at[at % BUFFERS, slot]
+        )
+
+    for slot in range(len(todo[0][1])):
+        products(0, slot)
     for at in range(len(todo) + 1):
-        if at + 1 < len(todo):
-            products(at + 1)
-        if at < len(todo):
-            buffer = at % BUFFERS
-            field_rows_step(work_x.at[buffer], work_z.at[buffer], len(todo[at][1]), rows_inv)
+        later = len(todo[at + 1][1]) if at + 1 < len(todo) else 0
+        now = len(todo[at][1]) if at < len(todo) else 0
+        for slot in range(max(later, now)):
+            if slot < later:
+                products(at + 1, slot)
+            if slot < now:
+                buffer = at % BUFFERS
+                field_rows_step(work_x.at[buffer, slot], work_z.at[buffer], slot, rows_inv)
         if at > 0:
             kernel, windows = todo[at - 1]
             pieces = field_cols_step(work_z.at[(at - 1) % BUFFERS], len(windows), cols_inv)
@@ -373,26 +377,23 @@
         jnp.concatenate([above[0:reach], below[0:reach]], axis=0),
         jnp.concatenate([second(above), second(below)], axis=0),
     )
+    last = windows - 1
     for side, window in enumerate(sides):
         mixed = right_dot(window, mask_cols)
+        span = slice(side * SIZE, (side + 1) * SIZE)
         for half_at, part in enumerate(split(mixed)):
             for phase in range(2):
                 cut = slice(phase * SIZE, (phase + 1) * SIZE)
                 base = phase * SIZE
-                span = slice(side * SIZE, (side + 1) * SIZE)
-                work_x[0, half_at, base:base + reach, span] = part[:reach, cut]
-                span = slice((2 + side) * SIZE, (3 + side) * SIZE)
-                work_x[0, half_at, base + STEP:base + SIZE, span] = part[reach:, cut]
+                work_x[0, 0, half_at, base:base + reach, span] = part[:reach, cut]
+                work_x[0, last, half_at, base + STEP:base + SIZE, span] = part[reach:, cut]
     for half_at in range(2):
         for phase in range(2):
             base = phase * SIZE
-            span = slice(0, 2 * SIZE)
-            work_x[0, half_at, base + reach:base + SIZE, span] = own_cols[half_at, phase, 0:STEP]
-            span = slice(2 * SIZE, 4 * SIZE)
-            work_x[0, half_at, base:base + STEP, span] = own_cols[half_at, phase, rows - STEP:]
-    outer = left_dot(rows_fwd, (work_x[0, 0, :, 0:4 * SIZE], work_x[0, 1, :, 0:4 * SIZE]))
-    mask_spec[0] = outer[:, 0:2 * SIZE]
-    mask_spec[1] = outer[:, 2 * SIZE:]
+            work_x[0, 0, half_at, base + reach:base + SIZE] = own_cols[half_at, phase, 0:STEP]
+            work_x[0, last, half_at, base:base + STEP] = own_cols[half_at, phase, rows - STEP:]
+    for index in (0, last):
+        mask_spec[index] = left_dot(rows_fwd, (work_x[0, index, 0], work_x[0, index, 1]))
 
     all_spectra([taps3[kernel] for kernel in range(late)], work_t, taps_cols, taps_rows, late_spectra)
 
@@ -409,7 +410,7 @@
 
     all_fields(
         [(kernel, (0, 2) if kernel < early else (0, 1, 2)) for kernel in range(count)],
-        spectra, {0: mask_spec.at[0], 1: mid_spec, 2: mask_spec.at[1]},
+        spectra, {0: mask_spec.at[0], 1: mid_spec, 2: mask_spec.at[2]},
         work_x, work_z, rows_inv, cols_inv, take,
     )
 
@@ -446,49 +447,40 @@
 
     grad_spec[...] = jnp.zeros_like(grad_spec)
 
-    def grad_cols_step(pair):
+    def grad_cols_step(pair, member):
         buffer = pair % BUFFERS
-        value = jnp.concatenate(
-            [slope[...] * field(2 * pair + member) for member in range(2)], axis=0
-        )
-        high, low = split(value)
-        mixed = dot(high, cols_fwd[0:256]) + (
-            dot(high, cols_fwd[256:]) + dot(low, cols_fwd[0:256])
-        )
+        span = slice(member * SIZE, (member + 1) * SIZE)
+        mixed = right_dot(slope[...] * field(2 * pair + member), cols_fwd)
         for half_at, part in enumerate(split(mixed)):
             for index in range(outs):
-                for member in range(2):
-                    base = member * field_rows + index * STEP
-                    at = slice(base, base + SIZE)
-                    base = (2 * index + member) * SIZE
-                    span = slice(base, base + SIZE)
-                    work_b[buffer, half_at, 0:SIZE, span] = part[at, :SIZE]
-                    work_b[buffer, half_at, SIZE:, span] = part[at, SIZE:]
-
-    def grad_rows_step(pair):
+                at = slice(index * STEP, index * STEP + SIZE)
+                work_b[buffer, index, half_at, 0:SIZE, span] = part[at, :SIZE]
+                work_b[buffer, index, half_at, SIZE:, span] = part[at, SIZE:]
+
+    def grad_rows_step(pair, index):
         buffer = pair % BUFFERS
-        spec = left_dot(rows_fwd, (work_b[buffer, 0], work_b[buffer, 1]))
-        for index in range(outs):
-            cut = slice(index * SIZE, (index + 1) * SIZE)
-            sum_re = grad_spec[0:SIZE, cut]
-            sum_im = grad_spec[SIZE:, cut]
-            for member in range(2):
-                base = (2 * index + member) * SIZE
-                span = slice(base, base + SIZE)
-                kern_re = spectra[2 * pair + member][0:SIZE]
-                kern_im = spectra[2 * pair + member][SIZE:]
-                spec_re = spec[0:SIZE, span]
-                spec_im = spec[SIZE:, span]
-                sum_re = sum_re + kern_re * spec_re + kern_im * spec_im
-                sum_im = sum_im + kern_re * spec_im - kern_im * spec_re
-            grad_spec[0:SIZE, cut] = sum_re
-            grad_spec[SIZE:, cut] = sum_im
+        spec = left_dot(rows_fwd, (work_b[buffer, index, 0], work_b[buffer, index, 1]))
+        cut = slice(index * SIZE, (index + 1) * SIZE)
+        sum_re = grad_spec[0:SIZE, cut]
+        sum_im = grad_spec[SIZE:, cut]
+        for member in range(2):
+            span = slice(member * SIZE, (member + 1) * SIZE)
+            kern_re = spectra[2 * pair + member][0:SIZE]
+            kern_im = spectra[2 * pair + member][SIZE:]
+            spec_re = spec[0:SIZE, span]
+            spec_im = spec[SIZE:, span]
+            sum_re = sum_re + kern_re * spec_re + kern_im * spec_im
+            sum_im = sum_im + kern_re * spec_im - kern_im * spec_re
+        grad_spec[0:SIZE, cut] = sum_re
+        grad_spec[SIZE:, cut] = sum_im
 
     for pair in range(pairs + 1):
-        if pair < pairs:
-            grad_cols_step(pair)
-        if pair > 0:
-            grad_rows_step(pair - 1)
+        for part in range(2):
+            if pair < pairs:
+                grad_cols_step(pair, part)
+            if pair > 0:
+                for index in range(part, outs, 2):
+                    grad_rows_step(pair - 1, index)
 
     halfway = left_dot(grad_rows, split(grad_spec[...]))
     stacked = jnp.concatenate(
@@ -576,7 +568,7 @@
         out_specs=(vmem,) * 5,
         scratch_shapes=[
             pltpu.VMEM((early * TAP_ROWS, 4 * SIZE), BF16),
-            pltpu.VMEM((BUFFERS, 2, 2 * SIZE, 2 * SIZE), BF16),
+            pltpu.VMEM((BUFFERS, 1, 2, 2 * SIZE, 2 * SIZE), BF16),
             pltpu.VMEM((BUFFERS, 2, 2 * STEP, 2 * SIZE), BF16),
         ],
         compiler_params=pltpu.CompilerParams(vmem_limit_bytes=16 * 1024 * 1024),
@@ -589,14 +581,14 @@
         out_specs=vmem,
         scratch_shapes=[
             pltpu.VMEM((local, 2 * SIZE, SIZE), F32),
-            pltpu.VMEM((2, 2 * SIZE, 2 * SIZE), F32),
+            pltpu.VMEM((windows, 2 * SIZE, 2 * SIZE), F32),
             pltpu.VMEM((count, field_rows, 2 * SIZE), F32),
             pltpu.VMEM((field_rows, 2 * SIZE), F32),
             pltpu.VMEM((field_rows, 2 * SIZE), F32),
             pltpu.VMEM((local * TAP_ROWS, 4 * SIZE), BF16),
-            pltpu.VMEM((BUFFERS, 2, 2 * SIZE, 2 * windows * SIZE), BF16),
+            pltpu.VMEM((BUFFERS, windows, 2, 2 * SIZE, 2 * SIZE), BF16),
             pltpu.VMEM((BUFFERS, 2, 2 * windows * STEP, 2 * SIZE), BF16),
-            pltpu.VMEM((BUFFERS, 2, 2 * SIZE, 2 * outs * SIZE), BF16),
+            pltpu.VMEM((BUFFERS, outs, 2, 2 * SIZE, 2 * SIZE), BF16),
             pltpu.VMEM((2 * SIZE, outs * SIZE), F32),
         ],
         compiler_params=pltpu.CompilerParams(vmem_limit_bytes=24 * 1024 * 1024),

time: 22.1 us -> 21.8 us (0.986)
  Pallas kernels: 14.5 us -> 14.2 us
    pallas_call x1, Pallas kernels: 9.27 us -> 9.01 us  [body(): pl.pallas_call(main_kernel, out_shape=jax.ShapeDtypeStruct((STEP, rows),...]
where the time goes in v1:
time: 21.8 us; the launch traced here: 21.7 us
  Pallas kernels  14.2 us (65%)
  starting transfers between devices  7.33 us (34%)
    pallas_call x1, Pallas kernels, body(): pl.pallas_call(main_kernel, out_shape=jax.ShapeDtypeStruct((STEP, rows),...  9.01 us
    ppermute x1, starting transfers between devices, body(): odd = lax.ppermute(odd, 'tile', swaps(1))  4.25 us
    ppermute x3, starting transfers between devices, flipped(): lax.ppermute(value, 'kern', [(i, i ^ flip) for i in range(kern_size)])  2.82 us
    pallas_call x1, Pallas kernels, body(): pl.pallas_call(local_kernel, out_shape=(jax.ShapeDtypeStruct((early, 2 *...  2.81 us
    pallas_call x1, Pallas kernels, body(): pl.pallas_call(pack_kernel, out_shape=(jax.ShapeDtypeStruct((2 * reach, S...  1.98 us
  transfers between devices with their start and end apart: 5, of which 0 were waited for; matrix products, arithmetic and copies ran while one was open for 0% of the time, Pallas kernels for 15%

profile of v1, /device:TPU:19, one launch (start us, length us, event | category | flops | bytes accessed | tf_op | source)
XLA Modules:
  0.0 21.7 jit_solution(16456161832720961328)
XLA Ops:
  0.0 2.0 %shard_map.55 = (f32[128,128]{1,0:T(8,128)}, f32[128,128]{1,0:T(8,128)}, f32[3,72,128]{2,1,0:T(8,128)}) custom-call(f32[3]{0:T(128)} %weight_ref.1, f32[128,256]{1,0:T(8,128)} %logit_ref.5, s32[128,256]{1,0:T(8,128)} %target_ref.3, f32[3,65,65]{2,1,0:T(8,128)} %real_ref.1, f32[3,65,65]{2,1,0:T(8,128)} %imag_ref.1), custom_call_target="tpu_custom_call" | custom-call | tf_op jit(solution)/shard_map/pallas_call | solution.py:523
  2.0 1.2 %collective-permute-start.2 = (f32[3,72,128]{2,1,0:T(8,128)}, f32[3,72,128]{2,1,0:T(8,128)S(1)}, u32[]{:S(2)}, u32[]{:S(2)}) collective-permute-start(f32[3,72,128]{2,1,0:T(8,128)} %get-tuple-element.15.taps0), channel_id=1, source_target_pairs={{0,2},{1,3},{2,0},{3,1},{4,6},{5,7},{6,4},{7,5},{8,10},{9,11},{10,... | collective-permute-start | bytes 331784 | tf_op jit(solution)/shard_map/ppermute | solution.py:538
  3.2 1.0 %collective-permute-start.4 = (f32[3,72,128]{2,1,0:T(8,128)}, f32[3,72,128]{2,1,0:T(8,128)S(1)}, u32[]{:S(2)}, u32[]{:S(2)}) collective-permute-start(f32[3,72,128]{2,1,0:T(8,128)} %get-tuple-element.15.taps0), channel_id=1, source_target_pairs={{0,1},{1,0},{2,3},{3,2},{4,5},{5,4},{6,7},{7,6},{8,9},{9,8},{10,11... | collective-permute-start | bytes 331784 | tf_op jit(solution)/shard_map/ppermute | solution.py:538
  4.2 0.3 %collective-permute-start = (f32[128,128]{1,0:T(8,128)}, f32[128,128]{1,0:T(8,128)S(1)}, u32[]{:S(2)}, u32[]{:S(2)}) collective-permute-start(f32[128,128]{1,0:T(8,128)} %get-tuple-element.13), channel_id=1, source_target_pairs={{0,4},{4,0},{8,12},{12,8},{16,20},{20,16},{24,28},{28,24},{1,5},{5... | collective-permute-start | bytes 196616 | tf_op jit(solution)/shard_map/ppermute | solution.py:542
  4.4 0.0 copy-start
  4.4 0.0 copy-start.2
  4.4 4.3 %collective-permute-start.1 = (f32[128,128]{1,0:T(8,128)}, f32[128,128]{1,0:T(8,128)S(1)}, u32[]{:S(2)}, u32[]{:S(2)}) collective-permute-start(f32[128,128]{1,0:T(8,128)} %get-tuple-element.14), channel_id=1, source_target_pairs={{4,8},{8,4},{12,16},{16,12},{20,24},{24,20},{5,9},{9,5},{13,17},{1... | collective-permute-start | bytes 196616 | tf_op jit(solution)/shard_map/ppermute | solution.py:543
  8.7 0.4 %shard_map.56.table_ref = bf16[3200,256]{1,0:T(8,128)(2,1)S(1)} custom-call(), custom_call_target="tpu_custom_call" | custom-call | flops 2000000000 | bytes 5000000 | tf_op jit(solution)/shard_map/pallas_call | solution.py:546
  9.1 0.0 copy-start.1
  9.1 0.0 collective-permute-done.2.taps2
  9.1 0.6 %collective-permute-start.3 = (f32[3,72,128]{2,1,0:T(8,128)S(1)}, f32[3,72,128]{2,1,0:T(8,128)S(1)}, u32[]{:S(2)}, u32[]{:S(2)}) collective-permute-start(f32[3,72,128]{2,1,0:T(8,128)S(1)} %collective-permute-done.2.taps2), channel_id=1, source_target_pairs={{0,1},{1,0},{2,3},{3,2},{4,5},{5,4},{6,7},{7,6},{8,9},{9,8},{10,11... | collective-permute-start | bytes 331784 | tf_op jit(solution)/shard_map/ppermute | solution.py:538
  9.8 0.0 collective-permute-done.4.taps1
  9.8 0.0 copy-done
  9.8 0.0 copy-done.2
  9.8 2.8 %shard_map.57 = (f32[9,256,128]{2,1,0:T(8,128)S(1)}, bf16[2,2,128,256]{3,2,1,0:T(8,128)(2,1)S(1)}, f32[256,256]{1,0:T(8,128)S(1)}, f32[9,64,256]{2,1,0:T(8,128)S(1)}, f32[64,256]{1,0:T(8,128)S(1)}) custom-call(f32[128,256]{1,0:T(8,128)S(1)} %copy-done, f32[3,72,128]{2,1,0:T(8,128)S(1)} %copy-done.2, f32[3,72,128]{2,1,0:T(8,128)S(1)} %collective-permute-done.4.taps1, ...), custom_call_target="tpu_custom_call" | custom-call | flops 4000000000 | bytes 5000000 | tf_op jit(solution)/shard_map/pallas_call | solution.py:558
  12.6 0.0 collective-permute-done.even_ref
  12.6 0.0 collective-permute-done.1.odd_ref
  12.6 0.0 collective-permute-done.3.taps3
  12.6 0.0 copy-done.1
  12.6 9.0 %shard_map.58 = f32[64,128]{1,0:T(8,128)} custom-call(f32[128,256]{1,0:T(8,128)S(1)} %copy-done, s32[128,256]{1,0:T(8,128)S(1)} %copy-done.1, f32[128,128]{1,0:T(8,128)S(1)} %collective-permute-done.even_ref, f32[128,128]{1,0:T(8,128)S(1)} %collective-permute-done.1.odd_ref, f32[3,72,128]{2,1,0:T(8,128)S(1)} %collective-permute-done.3.taps3, ...), custom_call_target="tpu_custom_call" | custom-call | tf_op jit(solution)/shard_map/pallas_call | solution.py:577
Async XLA Ops:
  2.0 7.2 %collective-permute-start.2 = (f32[3,72,128]{2,1,0:T(8,128)}, f32[3,72,128]{2,1,0:T(8,128)S(1)}, u32[]{:S(2)}, u32[]{:S(2)}) collective-permute-start(f32[3,72,128]{2,1,0:T(8,128)} %get-tuple-element.15.taps0), channel_id=1, source_target_pairs={{0,2},{1,3},{2,0},{3,1},{4,6},{5,7},{6,4},{7,5},{8,10},{9,11},{10,... | collective-permute-start | bytes 331784 | tf_op jit(solution)/shard_map/ppermute | solution.py:538
  3.2 6.6 %collective-permute-start.4 = (f32[3,72,128]{2,1,0:T(8,128)}, f32[3,72,128]{2,1,0:T(8,128)S(1)}, u32[]{:S(2)}, u32[]{:S(2)}) collective-permute-start(f32[3,72,128]{2,1,0:T(8,128)} %get-tuple-element.15.taps0), channel_id=1, source_target_pairs={{0,1},{1,0},{2,3},{3,2},{4,5},{5,4},{6,7},{7,6},{8,9},{9,8},{10,11... | collective-permute-start | bytes 331784 | tf_op jit(solution)/shard_map/ppermute | solution.py:538
  4.2 8.4 %collective-permute-start = (f32[128,128]{1,0:T(8,128)}, f32[128,128]{1,0:T(8,128)S(1)}, u32[]{:S(2)}, u32[]{:S(2)}) collective-permute-start(f32[128,128]{1,0:T(8,128)} %get-tuple-element.13), channel_id=1, source_target_pairs={{0,4},{4,0},{8,12},{12,8},{16,20},{20,16},{24,28},{28,24},{1,5},{5... | collective-permute-start | bytes 196616 | tf_op jit(solution)/shard_map/ppermute | solution.py:542
  4.4 5.3 %copy-start = (f32[128,256]{1,0:T(8,128)S(1)}, f32[128,256]{1,0:T(8,128)}, u32[]{:S(2)}) copy-start(f32[128,256]{1,0:T(8,128)} %logit_ref.5) | copy-start | bytes 393220
  4.4 5.3 %copy-start.2 = (f32[3,72,128]{2,1,0:T(8,128)S(1)}, f32[3,72,128]{2,1,0:T(8,128)}, u32[]{:S(2)}) copy-start(f32[3,72,128]{2,1,0:T(8,128)} %get-tuple-element.15.taps0) | copy-start | bytes 331780
  4.4 8.2 %collective-permute-start.1 = (f32[128,128]{1,0:T(8,128)}, f32[128,128]{1,0:T(8,128)S(1)}, u32[]{:S(2)}, u32[]{:S(2)}) collective-permute-start(f32[128,128]{1,0:T(8,128)} %get-tuple-element.14), channel_id=1, source_target_pairs={{4,8},{8,4},{12,16},{16,12},{20,24},{24,20},{5,9},{9,5},{13,17},{1... | collective-permute-start | bytes 196616 | tf_op jit(solution)/shard_map/ppermute | solution.py:543
  9.1 3.5 %copy-start.1 = (s32[128,256]{1,0:T(8,128)S(1)}, s32[128,256]{1,0:T(8,128)}, u32[]{:S(2)}) copy-start(s32[128,256]{1,0:T(8,128)} %target_ref.3) | copy-start | bytes 393220
  9.1 3.5 %collective-permute-start.3 = (f32[3,72,128]{2,1,0:T(8,128)S(1)}, f32[3,72,128]{2,1,0:T(8,128)S(1)}, u32[]{:S(2)}, u32[]{:S(2)}) collective-permute-start(f32[3,72,128]{2,1,0:T(8,128)S(1)} %collective-permute-done.2.taps2), channel_id=1, source_target_pairs={{0,1},{1,0},{2,3},{3,2},{4,5},{5,4},{6,7},{7,6},{8,9},{9,8},{10,11... | collective-permute-start | bytes 331784 | tf_op jit(solution)/shard_map/ppermute | solution.py:538

commit v2 on v1

--- a/solution.py
+++ b/solution.py
@@ -19,7 +19,7 @@
 F32 = jnp.float32
 BF16 = jnp.bfloat16
 TABLE_ROWS = (384, 512, 256, 512, 256, 256, 512, 256, 256)
-BUFFERS = 3
+BUFFERS = 6
 
 
 def table_views(ref):
@@ -336,7 +336,7 @@
     logit_ref, target_ref, even_ref, odd_ref, taps3, table_ref,
     early_spectra, own_cols, mid_spec, mid_fields, mid_total,
     out_ref,
-    late_spectra, mask_spec, fields, total, slope, work_t, work_x, work_z, work_b, grad_spec,
+    late_spectra, mask_spec, fields, total, slope, work_t, work_m, work_x, work_z, work_b, grad_spec,
 ):
     (
         taps_cols, taps_rows, mask_cols, rows_fwd, rows_inv, cols_inv, cols_fwd, grad_rows, grad_cols
@@ -385,15 +385,15 @@
             for phase in range(2):
                 cut = slice(phase * SIZE, (phase + 1) * SIZE)
                 base = phase * SIZE
-                work_x[0, 0, half_at, base:base + reach, span] = part[:reach, cut]
-                work_x[0, last, half_at, base + STEP:base + SIZE, span] = part[reach:, cut]
+                work_m[0, half_at, base:base + reach, span] = part[:reach, cut]
+                work_m[last, half_at, base + STEP:base + SIZE, span] = part[reach:, cut]
     for half_at in range(2):
         for phase in range(2):
             base = phase * SIZE
-            work_x[0, 0, half_at, base + reach:base + SIZE] = own_cols[half_at, phase, 0:STEP]
-            work_x[0, last, half_at, base:base + STEP] = own_cols[half_at, phase, rows - STEP:]
+            work_m[0, half_at, base + reach:base + SIZE] = own_cols[half_at, phase, 0:STEP]
+            work_m[last, half_at, base:base + STEP] = own_cols[half_at, phase, rows - STEP:]
     for index in (0, last):
-        mask_spec[index] = left_dot(rows_fwd, (work_x[0, index, 0], work_x[0, index, 1]))
+        mask_spec[index] = left_dot(rows_fwd, (work_m[index, 0], work_m[index, 1]))
 
     all_spectra([taps3[kernel] for kernel in range(late)], work_t, taps_cols, taps_rows, late_spectra)
 
@@ -586,12 +586,13 @@
             pltpu.VMEM((field_rows, 2 * SIZE), F32),
             pltpu.VMEM((field_rows, 2 * SIZE), F32),
             pltpu.VMEM((local * TAP_ROWS, 4 * SIZE), BF16),
+            pltpu.VMEM((windows, 2, 2 * SIZE, 2 * SIZE), BF16),
             pltpu.VMEM((BUFFERS, windows, 2, 2 * SIZE, 2 * SIZE), BF16),
             pltpu.VMEM((BUFFERS, 2, 2 * windows * STEP, 2 * SIZE), BF16),
             pltpu.VMEM((BUFFERS, outs, 2, 2 * SIZE, 2 * SIZE), BF16),
             pltpu.VMEM((2 * SIZE, outs * SIZE), F32),
         ],
-        compiler_params=pltpu.CompilerParams(vmem_limit_bytes=24 * 1024 * 1024),
+        compiler_params=pltpu.CompilerParams(vmem_limit_bytes=28 * 1024 * 1024),
     )(mask_logit, target, even, odd, both, table, *local_out)
     return jnp.transpose(result)
 

time: 21.8 us -> 22.3 us (1.023)
  Pallas kernels: 14.2 us -> 14.7 us
    pallas_call x1, Pallas kernels: 9.01 us -> 9.45 us  [body(): pl.pallas_call(main_kernel, out_shape=jax.ShapeDtypeStruct((STEP, rows),...]
where the time goes in v2:
time: 22.3 us; the launch traced here: 22.1 us
  Pallas kernels  14.7 us (66%)
  starting transfers between devices  7.33 us (33%)
    pallas_call x1, Pallas kernels, body(): pl.pallas_call(main_kernel, out_shape=jax.ShapeDtypeStruct((STEP, rows),...  9.45 us
    ppermute x1, starting transfers between devices, body(): odd = lax.ppermute(odd, 'tile', swaps(1))  4.25 us
    pallas_call x1, Pallas kernels, body(): pl.pallas_call(local_kernel, out_shape=(jax.ShapeDtypeStruct((early, 2 *...  2.87 us
    ppermute x3, starting transfers between devices, flipped(): lax.ppermute(value, 'kern', [(i, i ^ flip) for i in range(kern_size)])  2.82 us
    pallas_call x1, Pallas kernels, body(): pl.pallas_call(pack_kernel, out_shape=(jax.ShapeDtypeStruct((2 * reach, S...  1.98 us
  transfers between devices with their start and end apart: 5, of which 0 were waited for; matrix products, arithmetic and copies ran while one was open for 0% of the time, Pallas kernels for 15%

profile of v2, /device:TPU:19, one launch (start us, length us, event | category | flops | bytes accessed | tf_op | source)
XLA Modules:
  0.0 22.1 jit_solution(18411885231017961190)
XLA Ops:
  0.0 2.0 %shard_map.55 = (f32[128,128]{1,0:T(8,128)}, f32[128,128]{1,0:T(8,128)}, f32[3,72,128]{2,1,0:T(8,128)}) custom-call(f32[3]{0:T(128)} %weight_ref.1, f32[128,256]{1,0:T(8,128)} %logit_ref.5, s32[128,256]{1,0:T(8,128)} %target_ref.3, f32[3,65,65]{2,1,0:T(8,128)} %real_ref.1, f32[3,65,65]{2,1,0:T(8,128)} %imag_ref.1), custom_call_target="tpu_custom_call" | custom-call | tf_op jit(solution)/shard_map/pallas_call | solution.py:523
  2.0 1.2 %collective-permute-start.2 = (f32[3,72,128]{2,1,0:T(8,128)}, f32[3,72,128]{2,1,0:T(8,128)S(1)}, u32[]{:S(2)}, u32[]{:S(2)}) collective-permute-start(f32[3,72,128]{2,1,0:T(8,128)} %get-tuple-element.15.taps0), channel_id=1, source_target_pairs={{0,2},{1,3},{2,0},{3,1},{4,6},{5,7},{6,4},{7,5},{8,10},{9,11},{10,... | collective-permute-start | bytes 331784 | tf_op jit(solution)/shard_map/ppermute | solution.py:538
  3.2 1.0 %collective-permute-start.4 = (f32[3,72,128]{2,1,0:T(8,128)}, f32[3,72,128]{2,1,0:T(8,128)S(1)}, u32[]{:S(2)}, u32[]{:S(2)}) collective-permute-start(f32[3,72,128]{2,1,0:T(8,128)} %get-tuple-element.15.taps0), channel_id=1, source_target_pairs={{0,1},{1,0},{2,3},{3,2},{4,5},{5,4},{6,7},{7,6},{8,9},{9,8},{10,11... | collective-permute-start | bytes 331784 | tf_op jit(solution)/shard_map/ppermute | solution.py:538
  4.2 0.3 %collective-permute-start = (f32[128,128]{1,0:T(8,128)}, f32[128,128]{1,0:T(8,128)S(1)}, u32[]{:S(2)}, u32[]{:S(2)}) collective-permute-start(f32[128,128]{1,0:T(8,128)} %get-tuple-element.13), channel_id=1, source_target_pairs={{0,4},{4,0},{8,12},{12,8},{16,20},{20,16},{24,28},{28,24},{1,5},{5... | collective-permute-start | bytes 196616 | tf_op jit(solution)/shard_map/ppermute | solution.py:542
  4.4 0.0 copy-start
  4.4 0.0 copy-start.2
  4.4 4.3 %collective-permute-start.1 = (f32[128,128]{1,0:T(8,128)}, f32[128,128]{1,0:T(8,128)S(1)}, u32[]{:S(2)}, u32[]{:S(2)}) collective-permute-start(f32[128,128]{1,0:T(8,128)} %get-tuple-element.14), channel_id=1, source_target_pairs={{4,8},{8,4},{12,16},{16,12},{20,24},{24,20},{5,9},{9,5},{13,17},{1... | collective-permute-start | bytes 196616 | tf_op jit(solution)/shard_map/ppermute | solution.py:543
  8.7 0.4 %shard_map.56.table_ref = bf16[3200,256]{1,0:T(8,128)(2,1)S(1)} custom-call(), custom_call_target="tpu_custom_call" | custom-call | flops 2000000000 | bytes 5000000 | tf_op jit(solution)/shard_map/pallas_call | solution.py:546
  9.1 0.0 copy-start.1
  9.1 0.0 collective-permute-done.2.taps2
  9.1 0.6 %collective-permute-start.3 = (f32[3,72,128]{2,1,0:T(8,128)S(1)}, f32[3,72,128]{2,1,0:T(8,128)S(1)}, u32[]{:S(2)}, u32[]{:S(2)}) collective-permute-start(f32[3,72,128]{2,1,0:T(8,128)S(1)} %collective-permute-done.2.taps2), channel_id=1, source_target_pairs={{0,1},{1,0},{2,3},{3,2},{4,5},{5,4},{6,7},{7,6},{8,9},{9,8},{10,11... | collective-permute-start | bytes 331784 | tf_op jit(solution)/shard_map/ppermute | solution.py:538
  9.8 0.0 collective-permute-done.4.taps1
  9.8 0.0 copy-done
  9.8 0.0 copy-done.2
  9.8 2.9 %shard_map.57 = (f32[9,256,128]{2,1,0:T(8,128)S(1)}, bf16[2,2,128,256]{3,2,1,0:T(8,128)(2,1)S(1)}, f32[256,256]{1,0:T(8,128)S(1)}, f32[9,64,256]{2,1,0:T(8,128)S(1)}, f32[64,256]{1,0:T(8,128)S(1)}) custom-call(f32[128,256]{1,0:T(8,128)S(1)} %copy-done, f32[3,72,128]{2,1,0:T(8,128)S(1)} %copy-done.2, f32[3,72,128]{2,1,0:T(8,128)S(1)} %collective-permute-done.4.taps1, ...), custom_call_target="tpu_custom_call" | custom-call | flops 4000000000 | bytes 5000000 | tf_op jit(solution)/shard_map/pallas_call | solution.py:558
  12.7 0.0 collective-permute-done.even_ref
  12.7 0.0 collective-permute-done.1.odd_ref
  12.7 0.0 collective-permute-done.3.taps3
  12.7 0.0 copy-done.1
  12.7 9.4 %shard_map.58 = f32[64,128]{1,0:T(8,128)} custom-call(f32[128,256]{1,0:T(8,128)S(1)} %copy-done, s32[128,256]{1,0:T(8,128)S(1)} %copy-done.1, f32[128,128]{1,0:T(8,128)S(1)} %collective-permute-done.even_ref, f32[128,128]{1,0:T(8,128)S(1)} %collective-permute-done.1.odd_ref, f32[3,72,128]{2,1,0:T(8,128)S(1)} %collective-permute-done.3.taps3, ...), custom_call_target="tpu_custom_call" | custom-call | tf_op jit(solution)/shard_map/pallas_call | solution.py:577
Async XLA Ops:
  2.0 7.2 %collective-permute-start.2 = (f32[3,72,128]{2,1,0:T(8,128)}, f32[3,72,128]{2,1,0:T(8,128)S(1)}, u32[]{:S(2)}, u32[]{:S(2)}) collective-permute-start(f32[3,72,128]{2,1,0:T(8,128)} %get-tuple-element.15.taps0), channel_id=1, source_target_pairs={{0,2},{1,3},{2,0},{3,1},{4,6},{5,7},{6,4},{7,5},{8,10},{9,11},{10,... | collective-permute-start | bytes 331784 | tf_op jit(solution)/shard_map/ppermute | solution.py:538
  3.2 6.6 %collective-permute-start.4 = (f32[3,72,128]{2,1,0:T(8,128)}, f32[3,72,128]{2,1,0:T(8,128)S(1)}, u32[]{:S(2)}, u32[]{:S(2)}) collective-permute-start(f32[3,72,128]{2,1,0:T(8,128)} %get-tuple-element.15.taps0), channel_id=1, source_target_pairs={{0,1},{1,0},{2,3},{3,2},{4,5},{5,4},{6,7},{7,6},{8,9},{9,8},{10,11... | collective-permute-start | bytes 331784 | tf_op jit(solution)/shard_map/ppermute | solution.py:538
  4.2 8.5 %collective-permute-start = (f32[128,128]{1,0:T(8,128)}, f32[128,128]{1,0:T(8,128)S(1)}, u32[]{:S(2)}, u32[]{:S(2)}) collective-permute-start(f32[128,128]{1,0:T(8,128)} %get-tuple-element.13), channel_id=1, source_target_pairs={{0,4},{4,0},{8,12},{12,8},{16,20},{20,16},{24,28},{28,24},{1,5},{5... | collective-permute-start | bytes 196616 | tf_op jit(solution)/shard_map/ppermute | solution.py:542
  4.4 5.3 %copy-start = (f32[128,256]{1,0:T(8,128)S(1)}, f32[128,256]{1,0:T(8,128)}, u32[]{:S(2)}) copy-start(f32[128,256]{1,0:T(8,128)} %logit_ref.5) | copy-start | bytes 393220
  4.4 5.3 %copy-start.2 = (f32[3,72,128]{2,1,0:T(8,128)S(1)}, f32[3,72,128]{2,1,0:T(8,128)}, u32[]{:S(2)}) copy-start(f32[3,72,128]{2,1,0:T(8,128)} %get-tuple-element.15.taps0) | copy-start | bytes 331780
  4.4 8.2 %collective-permute-start.1 = (f32[128,128]{1,0:T(8,128)}, f32[128,128]{1,0:T(8,128)S(1)}, u32[]{:S(2)}, u32[]{:S(2)}) collective-permute-start(f32[128,128]{1,0:T(8,128)} %get-tuple-element.14), channel_id=1, source_target_pairs={{4,8},{8,4},{12,16},{16,12},{20,24},{24,20},{5,9},{9,5},{13,17},{1... | collective-permute-start | bytes 196616 | tf_op jit(solution)/shard_map/ppermute | solution.py:543
  9.1 3.6 %copy-start.1 = (s32[128,256]{1,0:T(8,128)S(1)}, s32[128,256]{1,0:T(8,128)}, u32[]{:S(2)}) copy-start(s32[128,256]{1,0:T(8,128)} %target_ref.3) | copy-start | bytes 393220
  9.1 3.5 %collective-permute-start.3 = (f32[3,72,128]{2,1,0:T(8,128)S(1)}, f32[3,72,128]{2,1,0:T(8,128)S(1)}, u32[]{:S(2)}, u32[]{:S(2)}) collective-permute-start(f32[3,72,128]{2,1,0:T(8,128)S(1)} %collective-permute-done.2.taps2), channel_id=1, source_target_pairs={{0,1},{1,0},{2,3},{3,2},{4,5},{5,4},{6,7},{7,6},{8,9},{9,8},{10,11... | collective-permute-start | bytes 331784 | tf_op jit(solution)/shard_map/ppermute | solution.py:538

commit v3 on v1

--- a/solution.py
+++ b/solution.py
@@ -238,8 +238,8 @@
         work[1, SIZE:, cut] = low
 
 
-def field_rows_step(work, work_z, index, rows_inv):
-    high, low = split(left_dot(rows_inv, (work[0], work[1])))
+def field_rows_store(result, work_z, index):
+    high, low = split(result)
     for side in range(2):
         cut = slice(side * SIZE, (side + 1) * SIZE)
         base = (index * 2 + side) * STEP
@@ -250,15 +250,12 @@
         work_z[1, at, SIZE:] = low[STEP:, cut]
 
 
-def field_cols_step(work_z, windows, cols_inv):
-    pieces = windows * 2
-    major = dot(work_z[0, 0:pieces * STEP], cols_inv[...])
-    minor = dot(work_z[1, 0:pieces * STEP], cols_inv[:, 0:SIZE])
-    result = major[:, 0:SIZE] + (major[:, SIZE:] + minor)
-    return [
-        [result[(index * 2 + side) * STEP:(index * 2 + side + 1) * STEP] for side in range(2)]
-        for index in range(windows)
-    ]
+def staggered(units):
+    waiting, active = list(units), []
+    while waiting or active:
+        if waiting:
+            active.append(waiting.pop(0))
+        active = [unit for unit in active if next(unit, True) is None]
 
 
 def all_spectra(blocks, work_t, taps_cols, taps_rows, out):
@@ -272,28 +269,33 @@
 
 
 def all_fields(todo, spectra, mask_specs, work_x, work_z, rows_inv, cols_inv, take):
-    def products(at, slot):
-        kernel, windows = todo[at]
-        field_products(
-            spectra[kernel], mask_specs[windows[slot]], work_x.at[at % BUFFERS, slot]
-        )
-
-    for slot in range(len(todo[0][1])):
-        products(0, slot)
-    for at in range(len(todo) + 1):
-        later = len(todo[at + 1][1]) if at + 1 < len(todo) else 0
-        now = len(todo[at][1]) if at < len(todo) else 0
-        for slot in range(max(later, now)):
-            if slot < later:
-                products(at + 1, slot)
-            if slot < now:
-                buffer = at % BUFFERS
-                field_rows_step(work_x.at[buffer, slot], work_z.at[buffer], slot, rows_inv)
-        if at > 0:
-            kernel, windows = todo[at - 1]
-            pieces = field_cols_step(work_z.at[(at - 1) % BUFFERS], len(windows), cols_inv)
-            for index, pair in zip(windows, pieces):
-                take(kernel, index, pair)
+    def unit(number, kernel, buffer, windows, slot):
+        work, rows = work_x.at[number % BUFFERS], work_z.at[buffer]
+        field_products(spectra[kernel], mask_specs[windows[slot]], work)
+        yield
+        result = left_dot(rows_inv, (work[0], work[1]))
+        yield
+        field_rows_store(result, rows, slot)
+        if slot + 1 < len(windows):
+            return
+        yield
+        pieces = len(windows) * 2 * STEP
+        major = dot(rows[0, 0:pieces], cols_inv[...])
+        minor = dot(rows[1, 0:pieces], cols_inv[:, 0:SIZE])
+        yield
+        result = major[:, 0:SIZE] + (major[:, SIZE:] + minor)
+        for index, window in enumerate(windows):
+            pair = [
+                result[(index * 2 + side) * STEP:(index * 2 + side + 1) * STEP]
+                for side in range(2)
+            ]
+            take(kernel, window, pair)
+
+    units = []
+    for at, (kernel, windows) in enumerate(todo):
+        for slot in range(len(windows)):
+            units.append(unit(len(units), kernel, at % BUFFERS, windows, slot))
+    staggered(units)
 
 
 def local_kernel(
@@ -385,15 +387,15 @@
             for phase in range(2):
                 cut = slice(phase * SIZE, (phase + 1) * SIZE)
                 base = phase * SIZE
-                work_x[0, 0, half_at, base:base + reach, span] = part[:reach, cut]
-                work_x[0, last, half_at, base + STEP:base + SIZE, span] = part[reach:, cut]
+                work_x[0, half_at, base:base + reach, span] = part[:reach, cut]
+                work_x[last, half_at, base + STEP:base + SIZE, span] = part[reach:, cut]
     for half_at in range(2):
         for phase in range(2):
             base = phase * SIZE
-            work_x[0, 0, half_at, base + reach:base + SIZE] = own_cols[half_at, phase, 0:STEP]
-            work_x[0, last, half_at, base:base + STEP] = own_cols[half_at, phase, rows - STEP:]
+            work_x[0, half_at, base + reach:base + SIZE] = own_cols[half_at, phase, 0:STEP]
+            work_x[last, half_at, base:base + STEP] = own_cols[half_at, phase, rows - STEP:]
     for index in (0, last):
-        mask_spec[index] = left_dot(rows_fwd, (work_x[0, index, 0], work_x[0, index, 1]))
+        mask_spec[index] = left_dot(rows_fwd, (work_x[index, 0], work_x[index, 1]))
 
     all_spectra([taps3[kernel] for kernel in range(late)], work_t, taps_cols, taps_rows, late_spectra)
 
@@ -447,40 +449,38 @@
 
     grad_spec[...] = jnp.zeros_like(grad_spec)
 
-    def grad_cols_step(pair, member):
-        buffer = pair % BUFFERS
+    def grad_unit(kernel):
+        pair, member = kernel // 2, kernel % 2
+        work = work_b.at[pair % BUFFERS]
         span = slice(member * SIZE, (member + 1) * SIZE)
-        mixed = right_dot(slope[...] * field(2 * pair + member), cols_fwd)
+        mixed = right_dot(slope[...] * field(kernel), cols_fwd)
+        yield
         for half_at, part in enumerate(split(mixed)):
             for index in range(outs):
                 at = slice(index * STEP, index * STEP + SIZE)
-                work_b[buffer, index, half_at, 0:SIZE, span] = part[at, :SIZE]
-                work_b[buffer, index, half_at, SIZE:, span] = part[at, SIZE:]
-
-    def grad_rows_step(pair, index):
-        buffer = pair % BUFFERS
-        spec = left_dot(rows_fwd, (work_b[buffer, index, 0], work_b[buffer, index, 1]))
-        cut = slice(index * SIZE, (index + 1) * SIZE)
-        sum_re = grad_spec[0:SIZE, cut]
-        sum_im = grad_spec[SIZE:, cut]
-        for member in range(2):
-            span = slice(member * SIZE, (member + 1) * SIZE)
-            kern_re = spectra[2 * pair + member][0:SIZE]
-            kern_im = spectra[2 * pair + member][SIZE:]
-            spec_re = spec[0:SIZE, span]
-            spec_im = spec[SIZE:, span]
-            sum_re = sum_re + kern_re * spec_re + kern_im * spec_im
-            sum_im = sum_im + kern_re * spec_im - kern_im * spec_re
-        grad_spec[0:SIZE, cut] = sum_re
-        grad_spec[SIZE:, cut] = sum_im
-
-    for pair in range(pairs + 1):
-        for part in range(2):
-            if pair < pairs:
-                grad_cols_step(pair, part)
-            if pair > 0:
-                for index in range(part, outs, 2):
-                    grad_rows_step(pair - 1, index)
+                work[index, half_at, 0:SIZE, span] = part[at, :SIZE]
+                work[index, half_at, SIZE:, span] = part[at, SIZE:]
+        if member == 0:
+            return
+        yield
+        for index in range(outs):
+            spec = left_dot(rows_fwd, (work[index, 0], work[index, 1]))
+            yield
+            cut = slice(index * SIZE, (index + 1) * SIZE)
+            sum_re = grad_spec[0:SIZE, cut]
+            sum_im = grad_spec[SIZE:, cut]
+            for late_member in range(2):
+                span = slice(late_member * SIZE, (late_member + 1) * SIZE)
+                kern_re = spectra[2 * pair + late_member][0:SIZE]
+                kern_im = spectra[2 * pair + late_member][SIZE:]
+                spec_re = spec[0:SIZE, span]
+                spec_im = spec[SIZE:, span]
+                sum_re = sum_re + kern_re * spec_re + kern_im * spec_im
+                sum_im = sum_im + kern_re * spec_im - kern_im * spec_re
+            grad_spec[0:SIZE, cut] = sum_re
+            grad_spec[SIZE:, cut] = sum_im
+
+    staggered(grad_unit(kernel) for kernel in range(count))
 
     halfway = left_dot(grad_rows, split(grad_spec[...]))
     stacked = jnp.concatenate(
@@ -568,7 +568,7 @@
         out_specs=(vmem,) * 5,
         scratch_shapes=[
             pltpu.VMEM((early * TAP_ROWS, 4 * SIZE), BF16),
-            pltpu.VMEM((BUFFERS, 1, 2, 2 * SIZE, 2 * SIZE), BF16),
+            pltpu.VMEM((BUFFERS, 2, 2 * SIZE, 2 * SIZE), BF16),
             pltpu.VMEM((BUFFERS, 2, 2 * STEP, 2 * SIZE), BF16),
         ],
         compiler_params=pltpu.CompilerParams(vmem_limit_bytes=16 * 1024 * 1024),
@@ -586,7 +586,7 @@
             pltpu.VMEM((field_rows, 2 * SIZE), F32),
             pltpu.VMEM((field_rows, 2 * SIZE), F32),
             pltpu.VMEM((local * TAP_ROWS, 4 * SIZE), BF16),
-            pltpu.VMEM((BUFFERS, windows, 2, 2 * SIZE, 2 * SIZE), BF16),
+            pltpu.VMEM((BUFFERS, 2, 2 * SIZE, 2 * SIZE), BF16),
             pltpu.VMEM((BUFFERS, 2, 2 * windows * STEP, 2 * SIZE), BF16),
             pltpu.VMEM((BUFFERS, outs, 2, 2 * SIZE, 2 * SIZE), BF16),
             pltpu.VMEM((2 * SIZE, outs * SIZE), F32),

time: 21.8 us -> 21.8 us (level)
  no operation moved by 1% of the time
where the time goes in v3:
time: 21.8 us; the launch traced here: 21.6 us
  Pallas kernels  14.2 us (65%)
  starting transfers between devices  7.33 us (34%)
    pallas_call x1, Pallas kernels, body(): pl.pallas_call(main_kernel, out_shape=jax.ShapeDtypeStruct((STEP, rows),...  8.99 us
    ppermute x1, starting transfers between devices, body(): odd = lax.ppermute(odd, 'tile', swaps(1))  4.25 us
    ppermute x3, starting transfers between devices, flipped(): lax.ppermute(value, 'kern', [(i, i ^ flip) for i in range(kern_size)])  2.82 us
    pallas_call x1, Pallas kernels, body(): pl.pallas_call(local_kernel, out_shape=(jax.ShapeDtypeStruct((early, 2 *...  2.81 us
    pallas_call x1, Pallas kernels, body(): pl.pallas_call(pack_kernel, out_shape=(jax.ShapeDtypeStruct((2 * reach, S...  1.98 us
  transfers between devices with their start and end apart: 5, of which 0 were waited for; matrix products, arithmetic and copies ran while one was open for 0% of the time, Pallas kernels for 15%

profile of v3, /device:TPU:19, one launch (start us, length us, event | category | flops | bytes accessed | tf_op | source)
XLA Modules:
  0.0 21.6 jit_solution(15705164237518484032)
XLA Ops:
  0.0 2.0 %shard_map.55 = (f32[128,128]{1,0:T(8,128)}, f32[128,128]{1,0:T(8,128)}, f32[3,72,128]{2,1,0:T(8,128)}) custom-call(f32[3]{0:T(128)} %weight_ref.1, f32[128,256]{1,0:T(8,128)} %logit_ref.5, s32[128,256]{1,0:T(8,128)} %target_ref.3, f32[3,65,65]{2,1,0:T(8,128)} %real_ref.1, f32[3,65,65]{2,1,0:T(8,128)} %imag_ref.1), custom_call_target="tpu_custom_call" | custom-call | tf_op jit(solution)/shard_map/pallas_call | solution.py:523
  2.0 1.2 %collective-permute-start.2 = (f32[3,72,128]{2,1,0:T(8,128)}, f32[3,72,128]{2,1,0:T(8,128)S(1)}, u32[]{:S(2)}, u32[]{:S(2)}) collective-permute-start(f32[3,72,128]{2,1,0:T(8,128)} %get-tuple-element.15.taps0), channel_id=1, source_target_pairs={{0,2},{1,3},{2,0},{3,1},{4,6},{5,7},{6,4},{7,5},{8,10},{9,11},{10,... | collective-permute-start | bytes 331784 | tf_op jit(solution)/shard_map/ppermute | solution.py:538
  3.2 1.0 %collective-permute-start.4 = (f32[3,72,128]{2,1,0:T(8,128)}, f32[3,72,128]{2,1,0:T(8,128)S(1)}, u32[]{:S(2)}, u32[]{:S(2)}) collective-permute-start(f32[3,72,128]{2,1,0:T(8,128)} %get-tuple-element.15.taps0), channel_id=1, source_target_pairs={{0,1},{1,0},{2,3},{3,2},{4,5},{5,4},{6,7},{7,6},{8,9},{9,8},{10,11... | collective-permute-start | bytes 331784 | tf_op jit(solution)/shard_map/ppermute | solution.py:538
  4.2 0.3 %collective-permute-start = (f32[128,128]{1,0:T(8,128)}, f32[128,128]{1,0:T(8,128)S(1)}, u32[]{:S(2)}, u32[]{:S(2)}) collective-permute-start(f32[128,128]{1,0:T(8,128)} %get-tuple-element.13), channel_id=1, source_target_pairs={{0,4},{4,0},{8,12},{12,8},{16,20},{20,16},{24,28},{28,24},{1,5},{5... | collective-permute-start | bytes 196616 | tf_op jit(solution)/shard_map/ppermute | solution.py:542
  4.4 0.0 copy-start
  4.4 0.0 copy-start.2
  4.4 4.3 %collective-permute-start.1 = (f32[128,128]{1,0:T(8,128)}, f32[128,128]{1,0:T(8,128)S(1)}, u32[]{:S(2)}, u32[]{:S(2)}) collective-permute-start(f32[128,128]{1,0:T(8,128)} %get-tuple-element.14), channel_id=1, source_target_pairs={{4,8},{8,4},{12,16},{16,12},{20,24},{24,20},{5,9},{9,5},{13,17},{1... | collective-permute-start | bytes 196616 | tf_op jit(solution)/shard_map/ppermute | solution.py:543
  8.7 0.4 %shard_map.56.table_ref = bf16[3200,256]{1,0:T(8,128)(2,1)S(1)} custom-call(), custom_call_target="tpu_custom_call" | custom-call | flops 2000000000 | bytes 5000000 | tf_op jit(solution)/shard_map/pallas_call | solution.py:546
  9.1 0.0 copy-start.1
  9.1 0.0 collective-permute-done.2.taps2
  9.1 0.6 %collective-permute-start.3 = (f32[3,72,128]{2,1,0:T(8,128)S(1)}, f32[3,72,128]{2,1,0:T(8,128)S(1)}, u32[]{:S(2)}, u32[]{:S(2)}) collective-permute-start(f32[3,72,128]{2,1,0:T(8,128)S(1)} %collective-permute-done.2.taps2), channel_id=1, source_target_pairs={{0,1},{1,0},{2,3},{3,2},{4,5},{5,4},{6,7},{7,6},{8,9},{9,8},{10,11... | collective-permute-start | bytes 331784 | tf_op jit(solution)/shard_map/ppermute | solution.py:538
  9.8 0.0 collective-permute-done.4.taps1
  9.8 0.0 copy-done
  9.8 0.0 copy-done.2
  9.8 2.8 %shard_map.57 = (f32[9,256,128]{2,1,0:T(8,128)S(1)}, bf16[2,2,128,256]{3,2,1,0:T(8,128)(2,1)S(1)}, f32[256,256]{1,0:T(8,128)S(1)}, f32[9,64,256]{2,1,0:T(8,128)S(1)}, f32[64,256]{1,0:T(8,128)S(1)}) custom-call(f32[128,256]{1,0:T(8,128)S(1)} %copy-done, f32[3,72,128]{2,1,0:T(8,128)S(1)} %copy-done.2, f32[3,72,128]{2,1,0:T(8,128)S(1)} %collective-permute-done.4.taps1, ...), custom_call_target="tpu_custom_call" | custom-call | flops 4000000000 | bytes 5000000 | tf_op jit(solution)/shard_map/pallas_call | solution.py:558
  12.6 0.0 collective-permute-done.even_ref
  12.6 0.0 collective-permute-done.1.odd_ref
  12.6 0.0 collective-permute-done.3.taps3
  12.6 0.0 copy-done.1
  12.6 9.0 %shard_map.58 = f32[64,128]{1,0:T(8,128)} custom-call(f32[128,256]{1,0:T(8,128)S(1)} %copy-done, s32[128,256]{1,0:T(8,128)S(1)} %copy-done.1, f32[128,128]{1,0:T(8,128)S(1)} %collective-permute-done.even_ref, f32[128,128]{1,0:T(8,128)S(1)} %collective-permute-done.1.odd_ref, f32[3,72,128]{2,1,0:T(8,128)S(1)} %collective-permute-done.3.taps3, ...), custom_call_target="tpu_custom_call" | custom-call | tf_op jit(solution)/shard_map/pallas_call | solution.py:577
Async XLA Ops:
  2.0 7.2 %collective-permute-start.2 = (f32[3,72,128]{2,1,0:T(8,128)}, f32[3,72,128]{2,1,0:T(8,128)S(1)}, u32[]{:S(2)}, u32[]{:S(2)}) collective-permute-start(f32[3,72,128]{2,1,0:T(8,128)} %get-tuple-element.15.taps0), channel_id=1, source_target_pairs={{0,2},{1,3},{2,0},{3,1},{4,6},{5,7},{6,4},{7,5},{8,10},{9,11},{10,... | collective-permute-start | bytes 331784 | tf_op jit(solution)/shard_map/ppermute | solution.py:538
  3.2 6.6 %collective-permute-start.4 = (f32[3,72,128]{2,1,0:T(8,128)}, f32[3,72,128]{2,1,0:T(8,128)S(1)}, u32[]{:S(2)}, u32[]{:S(2)}) collective-permute-start(f32[3,72,128]{2,1,0:T(8,128)} %get-tuple-element.15.taps0), channel_id=1, source_target_pairs={{0,1},{1,0},{2,3},{3,2},{4,5},{5,4},{6,7},{7,6},{8,9},{9,8},{10,11... | collective-permute-start | bytes 331784 | tf_op jit(solution)/shard_map/ppermute | solution.py:538
  4.2 8.4 %collective-permute-start = (f32[128,128]{1,0:T(8,128)}, f32[128,128]{1,0:T(8,128)S(1)}, u32[]{:S(2)}, u32[]{:S(2)}) collective-permute-start(f32[128,128]{1,0:T(8,128)} %get-tuple-element.13), channel_id=1, source_target_pairs={{0,4},{4,0},{8,12},{12,8},{16,20},{20,16},{24,28},{28,24},{1,5},{5... | collective-permute-start | bytes 196616 | tf_op jit(solution)/shard_map/ppermute | solution.py:542
  4.4 5.3 %copy-start = (f32[128,256]{1,0:T(8,128)S(1)}, f32[128,256]{1,0:T(8,128)}, u32[]{:S(2)}) copy-start(f32[128,256]{1,0:T(8,128)} %logit_ref.5) | copy-start | bytes 393220
  4.4 5.3 %copy-start.2 = (f32[3,72,128]{2,1,0:T(8,128)S(1)}, f32[3,72,128]{2,1,0:T(8,128)}, u32[]{:S(2)}) copy-start(f32[3,72,128]{2,1,0:T(8,128)} %get-tuple-element.15.taps0) | copy-start | bytes 331780
  4.4 8.2 %collective-permute-start.1 = (f32[128,128]{1,0:T(8,128)}, f32[128,128]{1,0:T(8,128)S(1)}, u32[]{:S(2)}, u32[]{:S(2)}) collective-permute-start(f32[128,128]{1,0:T(8,128)} %get-tuple-element.14), channel_id=1, source_target_pairs={{4,8},{8,4},{12,16},{16,12},{20,24},{24,20},{5,9},{9,5},{13,17},{1... | collective-permute-start | bytes 196616 | tf_op jit(solution)/shard_map/ppermute | solution.py:543
  9.1 3.5 %copy-start.1 = (s32[128,256]{1,0:T(8,128)S(1)}, s32[128,256]{1,0:T(8,128)}, u32[]{:S(2)}) copy-start(s32[128,256]{1,0:T(8,128)} %target_ref.3) | copy-start | bytes 393220
  9.1 3.5 %collective-permute-start.3 = (f32[3,72,128]{2,1,0:T(8,128)S(1)}, f32[3,72,128]{2,1,0:T(8,128)S(1)}, u32[]{:S(2)}, u32[]{:S(2)}) collective-permute-start(f32[3,72,128]{2,1,0:T(8,128)S(1)} %collective-permute-done.2.taps2), channel_id=1, source_target_pairs={{0,1},{1,0},{2,3},{3,2},{4,5},{5,4},{6,7},{7,6},{8,9},{9,8},{10,11... | collective-permute-start | bytes 331784 | tf_op jit(solution)/shard_map/ppermute | solution.py:538
